TPU v7x, 128 devices: a whole 4x4x4 slice. The times are simulated.
128 devices in a mesh: role: 2 (over y_hi), dev: 64 (over z, x, y_lo, core).
Axes of the slice: x: 4, y: 4 (y_hi: 2, y_lo: 2; y = y_hi * 2 + y_lo), z: 4, core: 2. Of those that a mesh axis runs over, the one named last changes fastest.
Arguments:
- tokens: bfloat16 [65536, 1024], P(('role', 'dev')), may hold values from -6 to 6
- expert_ids: int32 [65536, 1], P(('role', 'dev')), may hold values from 0 to 127; in each aligned block of 512 rows (0 to 511, 512 to 1023, ...) at most 8 rows name the same one
- w_qkv: bfloat16 [1024, 3072], P(('role', 'dev')), may hold values from -2 to 2
- w_attn_out: bfloat16 [1024, 1024], P(('role', 'dev')), may hold values from -0.1875 to 0.1875
- gain_attn: bfloat16 [1024], replicated, may hold values from 0.5 to 1.5
- gain_expert: bfloat16 [1024], replicated, may hold values from 0.5 to 1.5
- router: bfloat16 [1024, 128], replicated, may hold values from -0.375 to 0.375
- expert_in: bfloat16 [128, 1024, 2816], P(('role', 'dev')), may hold values from -0.1875 to 0.1875
- expert_out: bfloat16 [128, 2816, 1024], P(('role', 'dev')), may hold values from -0.109375 to 0.109375
- capacity: int32 [128], replicated, may hold values from 256 to 1023
- swap_list: int32 [32], replicated, may hold values from 0 to 63, as said below
Outputs:
- mixed: bfloat16 [65536, 1024], P(('role', 'dev'))
Inputs may be any that keep to these rules, and one draw needn't show every extreme that they name: `expert_ids`: in the rows of one device no expert is named more than 8 times, a bound that some block reaches. `swap_list`: entries are distinct.
All inputs are finite; a program needn't handle non-finite values.
Results may differ from a plain program's by a relative error of at most 0.0052.
Values may be sent and summed in bfloat16 or wider, within the bound.
A program may use at most 128 MiB of HBM per device.

v0:
```python
import jax
import jax.numpy as jnp
from jax import lax
from jax.sharding import PartitionSpec as P

HEADS = 16


def entering(value, axis, join, neutral):
    count, mine = (lax.axis_size(axis), lax.axis_index(axis))
    pieces = lax.all_gather(value, axis)
    total = jnp.full_like(value, 0) + jnp.asarray(neutral, value.dtype)

    def turn(position, total):
        longer = join(total, pieces[position])
        return jnp.where(position < mine, longer, total)

    return lax.fori_loop(0, count - 1, turn, total)


def swapped(value, axis, stride):
    mask = 2**stride
    pairs = [(source, source ^ mask) for source in range(lax.axis_size(axis))]
    return lax.ppermute(value, axis, pairs)


def rms_scale(values, gain_vector):
    mean_sq = jnp.mean(values * values, axis=-1, keepdims=True)
    return values * lax.rsqrt(mean_sq + 1e-06) * gain_vector.astype(jnp.float32)


def self_attend(qkv_rows, head_count):
    row_count = qkv_rows.shape[0]
    model_width = qkv_rows.shape[1] // 3
    head_size = model_width // head_count
    queries = qkv_rows[:, :model_width].reshape(row_count, head_count, head_size)
    keys_all = qkv_rows[:, model_width : 2 * model_width].reshape(row_count, head_count, head_size)
    values = qkv_rows[:, 2 * model_width :].reshape(row_count, head_count, head_size)
    scores = jnp.einsum(
        "shd,thd->hst", queries, keys_all, preferred_element_type=jnp.float32
    ) * head_size ** (-0.5)
    row_max = jnp.max(scores, axis=-1, keepdims=True)
    weights = jnp.exp(scores - row_max)
    soft_weights = (weights / jnp.sum(weights, axis=-1, keepdims=True)).astype(jnp.bfloat16)
    context = jnp.einsum("hst,thd->shd", soft_weights, values, preferred_element_type=jnp.float32)
    return context.reshape(row_count, model_width).astype(jnp.bfloat16)


def add_counts(earlier, later):
    return earlier + later


def shards(
    tokens,
    expert_ids,
    w_qkv,
    w_attn_out,
    gain_attn,
    gain_expert,
    router,
    expert_in,
    expert_out,
    capacity,
    swap_list,
):
    seq_len, model_width = tokens.shape
    residual = tokens.astype(jnp.float32)
    normed = rms_scale(residual, gain_attn).astype(jnp.bfloat16)
    columns = normed
    qkv_rows = jnp.dot(
        columns,
        lax.all_gather(w_qkv, ("role", "dev"), axis=0, tiled=True),
        preferred_element_type=jnp.float32,
    ).astype(jnp.bfloat16)
    context = self_attend(qkv_rows, HEADS)
    columns = context
    attended = jnp.dot(
        columns,
        lax.all_gather(w_attn_out, ("role", "dev"), axis=0, tiled=True),
        preferred_element_type=jnp.float32,
    )
    hidden = residual + attended
    normed_ffn = rms_scale(hidden, gain_expert).astype(jnp.bfloat16)
    logits = jnp.dot(normed_ffn, router, preferred_element_type=jnp.float32)
    experts_all = router.shape[1]
    dev_count = lax.axis_size("dev")
    chosen = expert_ids[:, 0]
    expert_range = jnp.arange(experts_all, dtype=jnp.int32)
    match = chosen[:, None] == expert_range[None, :]
    gate = jax.nn.sigmoid(jnp.sum(jnp.where(match, logits, 0.0), axis=1))
    counts = jnp.sum(match.astype(jnp.int32), axis=0)
    before = entering(counts, ("role", "dev"), add_counts, jnp.zeros_like(counts))
    row_ids = lax.broadcasted_iota(jnp.int32, (seq_len, seq_len), 0)
    col_ids = lax.broadcasted_iota(jnp.int32, (seq_len, seq_len), 1)
    strict_lower = (col_ids < row_ids).astype(jnp.bfloat16)
    rank_table = jnp.dot(
        strict_lower, match.astype(jnp.bfloat16), preferred_element_type=jnp.float32
    )
    local_rank = jnp.sum(jnp.where(match, rank_table, 0.0), axis=1).astype(jnp.int32)
    position = local_rank + jnp.sum(jnp.where(match, before[None, :], 0), axis=1)
    flagged = jnp.any(swap_list[:, None] == jnp.arange(dev_count, dtype=jnp.int32)[None, :], axis=0)
    dev_index = expert_range % dev_count
    role_index = expert_range // dev_count
    flag_expert = jnp.any(
        (dev_index[:, None] == jnp.arange(dev_count, dtype=jnp.int32)[None, :]) & flagged[None, :],
        axis=1,
    )
    location = jnp.where(flag_expert, (1 - role_index) * dev_count + dev_index, expert_range)
    cap_expert = jnp.sum(
        jnp.where(location[:, None] == expert_range[None, :], capacity[None, :], 0), axis=1
    )
    limit = jnp.sum(jnp.where(match, cap_expert[None, :], 0), axis=1)
    kept = position < limit
    slot_rows = max(2, 2 * seq_len // experts_all)
    partner_in, partner_out = swapped((expert_in, expert_out), "role", 0)
    mine_swaps = jnp.any(swap_list == lax.axis_index("dev"))
    weight_in = jnp.where(mine_swaps, partner_in[0], expert_in[0])
    weight_out = jnp.where(mine_swaps, partner_out[0], expert_out[0])
    token_dest = jnp.sum(jnp.where(match, location[None, :], 0), axis=1)
    slot_index = token_dest * slot_rows + local_rank
    buffer = (
        jnp.zeros((experts_all * slot_rows, model_width), jnp.bfloat16)
        .at[slot_index]
        .set(normed_ffn)
    )
    buffer = buffer.reshape(experts_all, slot_rows, model_width)
    received = lax.all_to_all(buffer, ("role", "dev"), split_axis=0, concat_axis=0, tiled=True)
    flat_rows = received.reshape(-1, model_width)
    activ = jnp.maximum(
        jnp.dot(flat_rows, weight_in, preferred_element_type=jnp.float32), 0.0
    ).astype(jnp.bfloat16)
    produced = jnp.dot(activ, weight_out, preferred_element_type=jnp.float32).astype(jnp.bfloat16)
    returned = lax.all_to_all(
        produced.reshape(received.shape), ("role", "dev"), split_axis=0, concat_axis=0, tiled=True
    )
    picked = returned.reshape(-1, model_width)[slot_index].astype(jnp.float32)
    mixed = hidden + jnp.where(kept, gate, 0.0)[:, None] * picked
    return mixed.astype(jnp.bfloat16)


def solution(mesh):
    return jax.shard_map(
        shards,
        mesh=mesh,
        in_specs=(
            P(("role", "dev"), None),
            P(("role", "dev"), None),
            P(("role", "dev"), None),
            P(("role", "dev"), None),
            P(),
            P(),
            P(),
            P(("role", "dev"), None, None),
            P(("role", "dev"), None, None),
            P(),
            P(),
        ),
        out_specs=P(("role", "dev"), None),
        check_vma=False,
    )
```

profile of v0, /device:TPU:1, one launch (start us, length us, event | category | flops | bytes accessed | tf_op | source)
XLA Modules:
  0.0 754.5 jit_solution(13278155795753660415)
XLA Ops:
  6.6 0.7 all-gather.5.cloned.1.call-update
  7.3 3.8 collective-permute-start.1
  11.2 0.1 collective-permute-start
  11.3 0.8 convert_reduce_fusion
  12.1 1.1 fusion.27
  13.2 1.5 fusion.15
  14.7 412.8 %all-gather.1 = s32[128,1,128]{2,1,0:T(1,128)S(1)} all-gather(s32[1,1,128]{2,1,0:T(1,128)S(1)} %bitcast.57), channel_id=2, replica_groups=mesh['role'=2,'dev'=64] {'role','dev'}, dimensions={0}, use_global_device_ids=true | all-gather | bytes 66048 | tf_op jit(solution)/shard_map/all_gather | solution.py:11
  427.5 5.1 while.14
  432.7 0.1 fusion.36
  432.8 0.1 fusion.35
  432.9 0.2 select_reduce_fusion.3
  433.1 0.1 select_reduce_fusion.2
  433.3 16.4 %all-gather.5.cloned.1.call-done = bf16[1024,3072]{1,0:T(8,128)(2,1)} async-done(((bf16[8,3072]{1,0:T(8,128)(2,1)}), bf16[1024,3072]{1,0:T(8,128)(2,1)}) %all-gather.5.cloned.1.call-update) | async-done | bytes 6291472 | tf_op jit(solution)/shard_map/all_gather | solution.py:72
  449.7 6.6 convolution_convert_fusion
  456.2 1.3 fusion.43
  457.5 2.3 copy.24
  459.8 1.3 copy.25
  461.1 1.3 copy.26
  462.4 10.1 %fusion.44 = (f32[16,512]{1,0:T(8,128)S(1)}, f32[16,512,512]{1,2,0:T(8,128)}) fusion(bf16[512,16,64]{0,2,1:T(8,128)(2,1)S(1)} %bitcast.46, bf16[512,16,64]{0,2,1:T(8,128)(2,1)} %bitcast.47), kind=kOutput, calls=%fused_computation.75 | convolution fusion | flops 549454336 | bytes 18907136 | tf_op jit(solution)/shard_map/sub | solution.py:43
  472.5 8.3 %fusion.21 = bf16[16,64,512]{2,1,0:T(8,128)(2,1)} fusion(bf16[512,16,64]{0,2,1:T(8,128)(2,1)S(1)} %bitcast.45, f32[16,512,512]{1,2,0:T(8,128)} %get-tuple-element.115, f32[16,512]{1,0:T(8,128)S(1)} %get-tuple-element.114), kind=kOutput, calls=%fused_computation.32 | convolution fusion | flops 545783808 | bytes 18907136 | tf_op jit(solution)/shard_map/hst,thd->shd/dot_general | solution.py:45
  480.8 163.3 %all-gather.7.cloned.1.call-done = bf16[1024,1024]{1,0:T(8,128)(2,1)} async-done(((bf16[8,1024]{1,0:T(8,128)(2,1)}), bf16[1024,1024]{1,0:T(8,128)(2,1)}) %all-gather.7.cloned.1.call-update) | async-done | bytes 2097168 | tf_op jit(solution)/shard_map/all_gather | solution.py:79
  644.2 3.3 multiply_reduce_fusion.1
  647.5 4.2 scatter_custom_fusion
  651.7 7.1 all-to-all-start
  658.7 0.6 compare_reduce_fusion
  659.4 29.5 %all-to-all-done = bf16[128,8,1024]{2,1,0:T(8,128)(2,1)S(1)} async-done(((bf16[128,8,1024]{2,1,0:T(8,128)(2,1)}), bf16[128,8,1024]{2,1,0:T(8,128)(2,1)S(1)}, u32[]{:S(2)}, u32[]{:S(2)}) %all-to-all-start) | async-done | bytes 2097184 | tf_op jit(solution)/shard_map/all_to_all | solution.py:127
  688.9 18.3 %convert_bitcast_fusion = bf16[128,8,1024]{2,1,0:T(8,128)(2,1)} fusion(bf16[1,2816,1024]{2,1,0:T(8,128)(2,1)} %collective-permute-done.1, bf16[1,2816,1024]{2,1,0:T(8,128)(2,1)} %param.21, pred[]{:T(512)} %compare_reduce_fusion, bf16[1,1024,2816]{2,1,0:T(8,128)(2,1)} %collective-permute-done, bf16[1,1024,2816]{2,1,0:T(8,128)(2,1)} %param.20, ...), kind=kOutput, calls=%fused_computation.29 | convolution fusion | flops 11823742976 | bytes 27262976 | tf_op jit(solution)/shard_map/dot_general | solution.py:132
  707.2 5.4 all-to-all-start.1
  712.7 2.2 fusion.26
  714.9 27.9 %all-to-all-done.1 = bf16[128,8,1024]{2,1,0:T(8,128)(2,1)S(1)} async-done(((bf16[128,8,1024]{2,1,0:T(8,128)(2,1)}), bf16[128,8,1024]{2,1,0:T(8,128)(2,1)S(1)}, u32[]{:S(2)}, u32[]{:S(2)}) %all-to-all-start.1) | async-done | bytes 2097184 | tf_op jit(solution)/shard_map/all_to_all | solution.py:133
  742.8 2.0 gather_fusion
  744.8 2.9 add_convert_fusion
  (163 shorter events, 2.4 us)
Async XLA Ops:
  6.5 706.1 %copy-start = (bf16[1024,128]{1,0:T(8,128)(2,1)S(1)}, bf16[1024,128]{1,0:T(8,128)(2,1)}, u32[]{:S(2)}) copy-start(bf16[1024,128]{1,0:T(8,128)(2,1)} %param.19) | copy-start | bytes 786436
  6.5 426.5 %copy-start.5 = (s32[512,1]{0,1:T(1,128)S(1)}, s32[512,1]{0,1:T(1,128)}, u32[]{:S(2)}) copy-start(s32[512,1]{0,1:T(1,128)} %param.14) | copy-start | bytes 6148
  6.5 443.1 %copy-start.2 = (bf16[512,1024]{1,0:T(8,128)(2,1)S(1)}, bf16[512,1024]{1,0:T(8,128)(2,1)}, u32[]{:S(2)}) copy-start(bf16[512,1024]{1,0:T(8,128)(2,1)} %param.13) | copy-start | bytes 3145732
  6.5 426.1 %copy-start.9 = (s32[32]{0:T(128)S(1)}, s32[32]{0:T(128)}, u32[]{:S(2)}) copy-start(s32[32]{0:T(128)} %param.23) | copy-start | bytes 388
  6.5 426.3 %copy-start.8 = (s32[128]{0:T(128)S(1)}, s32[128]{0:T(128)}, u32[]{:S(2)}) copy-start(s32[128]{0:T(128)} %param.22) | copy-start | bytes 1540
  6.5 426.7 %copy-start.6 = (bf16[1024]{0:T(1024)(128)(2,1)S(1)}, bf16[1024]{0:T(1024)(128)(2,1)}, u32[]{:S(2)}) copy-start(bf16[1024]{0:T(1024)(128)(2,1)} %param.17) | copy-start | bytes 6148
  6.6 426.7 %copy-start.7 = (bf16[1024]{0:T(1024)(128)(2,1)S(1)}, bf16[1024]{0:T(1024)(128)(2,1)}, u32[]{:S(2)}) copy-start(bf16[1024]{0:T(1024)(128)(2,1)} %param.18) | copy-start | bytes 6148
  6.6 443.1 %all-gather.5.cloned.1.call-start = ((), (), s32[]{:S(2)}) async-start(), calls=%async_computation.2 | async-start | bytes 6340608 | tf_op jit(solution)/shard_map/all_gather | solution.py:72
  7.3 636.9 %all-gather.7.cloned.1.call-start = ((), (), s32[]{:S(2)}) async-start(), calls=%async_computation.3 | async-start | bytes 2113536 | tf_op jit(solution)/shard_map/all_gather | solution.py:79
  7.3 652.0 %collective-permute-start.1 = (bf16[1,2816,1024]{2,1,0:T(8,128)(2,1)}, bf16[1,2816,1024]{2,1,0:T(8,128)(2,1)}, u32[]{:S(2)}, u32[]{:S(2)}) collective-permute-start(bf16[1,2816,1024]{2,1,0:T(8,128)(2,1)} %param.21), channel_id=1, source_target_pairs={{0,64},{64,0},{1,65},{65,1},{2,66},{66,2},{3,67},{67,3},{4,68},{68... | collective-permute-start | bytes 17301512 | tf_op jit(solution)/shard_map/ppermute | solution.py:24
  11.2 648.2 %collective-permute-start = (bf16[1,1024,2816]{2,1,0:T(8,128)(2,1)}, bf16[1,1024,2816]{2,1,0:T(8,128)(2,1)}, u32[]{:S(2)}, u32[]{:S(2)}) collective-permute-start(bf16[1,1024,2816]{2,1,0:T(8,128)(2,1)} %param.20), channel_id=1, source_target_pairs={{0,64},{64,0},{1,65},{65,1},{2,66},{66,2},{3,67},{67,3},{4,68},{68... | collective-permute-start | bytes 17301512 | tf_op jit(solution)/shard_map/ppermute | solution.py:24
  461.1 1.3 copy-start.4
  462.4 10.1 %copy-start.3 = (bf16[512,1024]{0,1:T(8,128)(2,1)S(1)}, bf16[512,1024]{0,1:T(8,128)(2,1)}, u32[]{:S(2)}) copy-start(bf16[512,1024]{0,1:T(8,128)(2,1)} %copy.24) | copy-start | bytes 3145732
  647.4 4.2 copy-start.1
  651.7 37.2 %all-to-all-start = ((bf16[128,8,1024]{2,1,0:T(8,128)(2,1)}), bf16[128,8,1024]{2,1,0:T(8,128)(2,1)S(1)}, u32[]{:S(2)}, u32[]{:S(2)}) async-start(bf16[128,8,1024]{2,1,0:T(8,128)(2,1)} %bitcast.44), calls=%async_computation | async-start | bytes 4194304 | tf_op jit(solution)/shard_map/all_to_all | solution.py:127
  707.2 35.6 %all-to-all-start.1 = ((bf16[128,8,1024]{2,1,0:T(8,128)(2,1)}), bf16[128,8,1024]{2,1,0:T(8,128)(2,1)S(1)}, u32[]{:S(2)}, u32[]{:S(2)}) async-start(bf16[128,8,1024]{2,1,0:T(8,128)(2,1)} %convert_bitcast_fusion), calls=%async_computation.1 | async-start | bytes 4194304 | tf_op jit(solution)/shard_map/all_to_all | solution.py:133
Sparse Core Ops, SparseCore 0:
  9.1 440.4 all-gather.4
  451.4 192.7 all-gather.6
where the time goes:
time: 755 us
  blocking collectives  413 us (55%)
  waiting for transfers between devices  238 us (32%)
  matrix products  49.8 us (7%)
  starting transfers between devices  16.5 us (2%)
  between operations  13.6 us (2%)
  other arithmetic  12.8 us (2%)
  local copies, waits for them, and re-layouts  8.29 us (1%)
    all_gather x1, blocking collectives, entering(): pieces = lax.all_gather(value, axis)  413 us
    all_gather x1, waiting for transfers between devices, shards(): lax.all_gather(w_attn_out, ('role', 'dev'), axis=0, tiled=True)  163 us
    all_to_all x1, waiting for transfers between devices, shards(): lax.all_to_all(buffer, ('role', 'dev'), split_axis=0, concat_axis=0, tile...  29.5 us
    all_to_all x1, waiting for transfers between devices, shards(): lax.all_to_all(produced.reshape(received.shape), ('role', 'dev'), split_a...  27.9 us
    dot_general x1, matrix products, shards(): jnp.dot(activ, weight_out, preferred_element_type=jnp.float32)  18.3 us
    all_gather x1, waiting for transfers between devices, shards(): lax.all_gather(w_qkv, ('role', 'dev'), axis=0, tiled=True)  16.4 us
  transfers between devices with their start and end apart: 6, of which 4 were waited for; matrix products, arithmetic and copies ran while one was open for 6% of the time, Pallas kernels for 0%

commit v1 on v0

--- a/solution.py
+++ b/solution.py
@@ -69,7 +69,12 @@
     columns = normed
     qkv_rows = jnp.dot(
         columns,
-        lax.all_gather(w_qkv, ("role", "dev"), axis=0, tiled=True),
+        jnp.concatenate(
+            lax.all_to_all(
+                jnp.stack([w_qkv] * lax.axis_size(("role", "dev"))), ("role", "dev"), 0, 0
+            ),
+            axis=0,
+        ),
         preferred_element_type=jnp.float32,
     ).astype(jnp.bfloat16)
     context = self_attend(qkv_rows, HEADS)

time: 755 us -> 656 us (0.87)
  waiting for transfers between devices: 238 us -> 57.9 us
  blocking collectives: 413 us -> 483 us
  starting transfers between devices: 16.5 us -> 25.2 us
    all_gather x1, waiting for transfers between devices: 163 us -> 0.01 us  [shards(): lax.all_gather(w_attn_out, ('role', 'dev'), axis=0, tiled=True)]
    all_gather x1, blocking collectives: 413 us -> 483 us  [entering(): pieces = lax.all_gather(value, axis)]
    all_gather x1 -> x0, waiting for transfers between devices: 16.4 us -> none  [shards(): lax.all_gather(w_qkv, ('role', 'dev'), axis=0, tiled=True)]
    all_to_all x0 -> x1, starting transfers between devices: none -> 11.9 us  [shards(): lax.all_to_all(jnp.stack([w_qkv] * lax.axis_size(('role', 'dev'))), ('rol...]
  transfers between devices with their start and end apart: 6 -> 6, of which waited for: 4 -> 2; matrix products, arithmetic and copies ran while one was open for 6% -> 7% of each run, Pallas kernels for 0% -> 0%
where the time goes in v1:
time: 656 us; the launch traced here: 655 us
  blocking collectives  483 us (74%)
  waiting for transfers between devices  57.9 us (9%)
  matrix products  49.7 us (8%)
  starting transfers between devices  25.2 us (4%)
  between operations  13.6 us (2%)
  local copies, waits for them, and re-layouts  11.8 us (2%)
  other arithmetic  10.9 us (2%)
    all_gather x1, blocking collectives, entering(): pieces = lax.all_gather(value, axis)  483 us
    all_to_all x1, waiting for transfers between devices, shards(): lax.all_to_all(buffer, ('role', 'dev'), split_axis=0, concat_axis=0, tile...  29.3 us
    all_to_all x1, waiting for transfers between devices, shards(): lax.all_to_all(produced.reshape(received.shape), ('role', 'dev'), split_a...  27.9 us
    dot_general x1, matrix products, shards(): jnp.dot(activ, weight_out, preferred_element_type=jnp.float32)  19 us
  transfers between devices with their start and end apart: 6, of which 2 were waited for; matrix products, arithmetic and copies ran while one was open for 7% of the time, Pallas kernels for 0%

profile of v1, /device:TPU:1, one launch (start us, length us, event | category | flops | bytes accessed | tf_op | source)
XLA Modules:
  0.0 655.3 jit_solution(17092298329519748894)
XLA Ops:
  6.5 4.3 stack.2
  10.9 11.9 %all-to-all-start = ((bf16[128,8,3072]{2,1,0:T(8,128)(2,1)}), bf16[128,8,3072]{2,1,0:T(8,128)(2,1)}, u32[]{:S(2)}, u32[]{:S(2)}) async-start(bf16[128,8,3072]{2,1,0:T(8,128)(2,1)} %stack.2), calls=%async_computation | async-start | bytes 12582912 | tf_op jit(solution)/shard_map/all_to_all | solution.py:73
  22.8 0.7 all-gather.4.cloned.1.call-update
  23.5 3.0 collective-permute-start.1
  26.5 0.1 collective-permute-start
  26.6 0.1 convert_reduce_fusion
  26.7 483.4 %all-gather.1 = s32[128,1,128]{2,1,0:T(1,128)S(1)} all-gather(s32[1,1,128]{2,1,0:T(1,128)S(1)} %bitcast.61), channel_id=2, replica_groups=mesh['role'=2,'dev'=64] {'role','dev'}, dimensions={0}, use_global_device_ids=true | all-gather | bytes 66048 | tf_op jit(solution)/shard_map/all_gather | solution.py:11
  510.1 5.1 while.14
  515.3 0.1 fusion.41
  515.3 0.1 fusion.40
  515.5 0.2 select_reduce_fusion.3
  515.6 0.2 select_reduce_fusion.2
  515.8 0.3 fusion.32
  516.1 0.3 fusion.20
  516.5 6.6 %fusion.15 = bf16[512,3072]{1,0:T(8,128)(2,1)S(1)} fusion(bf16[128,8,3072]{2,1,0:T(8,128)(2,1)} %all-to-all-done, bf16[512,1024]{1,0:T(8,128)(2,1)S(1)} %copy-done.2, f32[1024]{0:T(1024)S(1)} %convert_element_type.62, f32[512]{0:T(512)S(1)} %add_rsqrt_fusion.1), kind=kOutput, calls=%fused_computation.21 | convolution fusion | flops 3224895488 | bytes 10491904 | tf_op jit(solution)/shard_map/dot_general | solution.py:70
  523.1 1.3 fusion.48
  524.3 2.3 copy.24
  526.6 1.3 copy.25
  527.9 0.5 copy.26
  528.5 10.1 %fusion.49 = (f32[16,512]{1,0:T(8,128)S(1)}, f32[16,512,512]{1,2,0:T(8,128)}) fusion(bf16[512,16,64]{0,2,1:T(8,128)(2,1)} %bitcast.50, bf16[512,16,64]{0,2,1:T(8,128)(2,1)S(1)} %bitcast.51), kind=kOutput, calls=%fused_computation.77 | convolution fusion | flops 549454336 | bytes 18907136 | tf_op jit(solution)/shard_map/sub | solution.py:43
  538.6 8.3 %fusion.26 = bf16[16,64,512]{2,1,0:T(8,128)(2,1)} fusion(bf16[512,16,64]{0,2,1:T(8,128)(2,1)S(1)} %bitcast.49, f32[16,512,512]{1,2,0:T(8,128)} %get-tuple-element.115, f32[16,512]{1,0:T(8,128)S(1)} %get-tuple-element.114), kind=kOutput, calls=%fused_computation.34 | convolution fusion | flops 545783808 | bytes 18907136 | tf_op jit(solution)/shard_map/hst,thd->shd/dot_general | solution.py:45
  546.9 3.3 multiply_reduce_fusion.1
  550.2 4.2 scatter_custom_fusion
  554.4 4.7 all-to-all-start.1
  559.2 0.6 compare_reduce_fusion
  559.8 29.3 %all-to-all-done.1 = bf16[128,8,1024]{2,1,0:T(8,128)(2,1)} async-done(((bf16[128,8,1024]{2,1,0:T(8,128)(2,1)}), bf16[128,8,1024]{2,1,0:T(8,128)(2,1)}, u32[]{:S(2)}, u32[]{:S(2)}) %all-to-all-start.1) | async-done | bytes 2097184 | tf_op jit(solution)/shard_map/all_to_all | solution.py:132
  589.1 19.0 %convert_bitcast_fusion = bf16[128,8,1024]{2,1,0:T(8,128)(2,1)} fusion(bf16[1,2816,1024]{2,1,0:T(8,128)(2,1)} %collective-permute-done.1, bf16[1,2816,1024]{2,1,0:T(8,128)(2,1)} %param.21, pred[]{:T(512)} %compare_reduce_fusion, bf16[1,1024,2816]{2,1,0:T(8,128)(2,1)} %collective-permute-done, bf16[1,1024,2816]{2,1,0:T(8,128)(2,1)} %param.20, ...), kind=kOutput, calls=%fused_computation.31 | convolution fusion | flops 11823742976 | bytes 27262976 | tf_op jit(solution)/shard_map/dot_general | solution.py:137
  608.0 5.4 all-to-all-start.2
  613.5 2.2 fusion.31
  615.7 27.9 %all-to-all-done.2 = bf16[128,8,1024]{2,1,0:T(8,128)(2,1)S(1)} async-done(((bf16[128,8,1024]{2,1,0:T(8,128)(2,1)}), bf16[128,8,1024]{2,1,0:T(8,128)(2,1)S(1)}, u32[]{:S(2)}, u32[]{:S(2)}) %all-to-all-start.2) | async-done | bytes 2097184 | tf_op jit(solution)/shard_map/all_to_all | solution.py:138
  643.6 2.0 gather_fusion
  645.6 2.9 add_convert_fusion
  (161 shorter events, 2.4 us)
Async XLA Ops:
  6.5 606.9 %copy-start = (bf16[1024,128]{1,0:T(8,128)(2,1)S(1)}, bf16[1024,128]{1,0:T(8,128)(2,1)}, u32[]{:S(2)}) copy-start(bf16[1024,128]{1,0:T(8,128)(2,1)} %param.19) | copy-start | bytes 786436
  10.8 15.8 %copy-start.4 = (s32[512,1]{0,1:T(1,128)S(1)}, s32[512,1]{0,1:T(1,128)}, u32[]{:S(2)}) copy-start(s32[512,1]{0,1:T(1,128)} %param.14) | copy-start | bytes 6148
  10.8 504.4 %copy-start.8 = (s32[32]{0:T(128)S(1)}, s32[32]{0:T(128)}, u32[]{:S(2)}) copy-start(s32[32]{0:T(128)} %param.23) | copy-start | bytes 388
  10.8 504.6 %copy-start.7 = (s32[128]{0:T(128)S(1)}, s32[128]{0:T(128)}, u32[]{:S(2)}) copy-start(s32[128]{0:T(128)} %param.22) | copy-start | bytes 1540
  10.8 505.3 %copy-start.2 = (bf16[512,1024]{1,0:T(8,128)(2,1)S(1)}, bf16[512,1024]{1,0:T(8,128)(2,1)}, u32[]{:S(2)}) copy-start(bf16[512,1024]{1,0:T(8,128)(2,1)} %param.13) | copy-start | bytes 3145732
  10.8 505.6 %copy-start.5 = (bf16[1024]{0:T(1024)(128)(2,1)S(1)}, bf16[1024]{0:T(1024)(128)(2,1)}, u32[]{:S(2)}) copy-start(bf16[1024]{0:T(1024)(128)(2,1)} %param.17) | copy-start | bytes 6148
  10.8 505.6 %copy-start.6 = (bf16[1024]{0:T(1024)(128)(2,1)S(1)}, bf16[1024]{0:T(1024)(128)(2,1)}, u32[]{:S(2)}) copy-start(bf16[1024]{0:T(1024)(128)(2,1)} %param.18) | copy-start | bytes 6148
  10.9 505.6 %all-to-all-start = ((bf16[128,8,3072]{2,1,0:T(8,128)(2,1)}), bf16[128,8,3072]{2,1,0:T(8,128)(2,1)}, u32[]{:S(2)}, u32[]{:S(2)}) async-start(bf16[128,8,3072]{2,1,0:T(8,128)(2,1)} %stack.2), calls=%async_computation | async-start | bytes 12582912 | tf_op jit(solution)/shard_map/all_to_all | solution.py:73
  22.8 524.1 %all-gather.4.cloned.1.call-start = ((), (), s32[]{:S(2)}) async-start(), calls=%async_computation.3 | async-start | bytes 2113536 | tf_op jit(solution)/shard_map/all_gather | solution.py:84
  23.5 536.3 %collective-permute-start.1 = (bf16[1,2816,1024]{2,1,0:T(8,128)(2,1)}, bf16[1,2816,1024]{2,1,0:T(8,128)(2,1)}, u32[]{:S(2)}, u32[]{:S(2)}) collective-permute-start(bf16[1,2816,1024]{2,1,0:T(8,128)(2,1)} %param.21), channel_id=1, source_target_pairs={{0,64},{64,0},{1,65},{65,1},{2,66},{66,2},{3,67},{67,3},{4,68},{68... | collective-permute-start | bytes 17301512 | tf_op jit(solution)/shard_map/ppermute | solution.py:24
  26.5 533.3 %collective-permute-start = (bf16[1,1024,2816]{2,1,0:T(8,128)(2,1)}, bf16[1,1024,2816]{2,1,0:T(8,128)(2,1)}, u32[]{:S(2)}, u32[]{:S(2)}) collective-permute-start(bf16[1,1024,2816]{2,1,0:T(8,128)(2,1)} %param.20), channel_id=1, source_target_pairs={{0,64},{64,0},{1,65},{65,1},{2,66},{66,2},{3,67},{67,3},{4,68},{68... | collective-permute-start | bytes 17301512 | tf_op jit(solution)/shard_map/ppermute | solution.py:24
  528.5 10.1 %copy-start.3 = (bf16[512,1024]{0,1:T(8,128)(2,1)S(1)}, bf16[512,1024]{0,1:T(8,128)(2,1)}, u32[]{:S(2)}) copy-start(bf16[512,1024]{0,1:T(8,128)(2,1)} %copy.24) | copy-start | bytes 3145732
  550.2 4.3 copy-start.1
  554.4 34.6 %all-to-all-start.1 = ((bf16[128,8,1024]{2,1,0:T(8,128)(2,1)}), bf16[128,8,1024]{2,1,0:T(8,128)(2,1)}, u32[]{:S(2)}, u32[]{:S(2)}) async-start(bf16[128,8,1024]{2,1,0:T(8,128)(2,1)} %bitcast.48), calls=%async_computation.1 | async-start | bytes 4194304 | tf_op jit(solution)/shard_map/all_to_all | solution.py:132
  608.0 35.6 %all-to-all-start.2 = ((bf16[128,8,1024]{2,1,0:T(8,128)(2,1)}), bf16[128,8,1024]{2,1,0:T(8,128)(2,1)S(1)}, u32[]{:S(2)}, u32[]{:S(2)}) async-start(bf16[128,8,1024]{2,1,0:T(8,128)(2,1)} %convert_bitcast_fusion), calls=%async_computation.2 | async-start | bytes 4194304 | tf_op jit(solution)/shard_map/all_to_all | solution.py:138
Sparse Core Ops, SparseCore 0:
  25.3 477.7 all-gather.3
